TPU v7x, 32 devices: a whole 2x2x4 slice. The times are simulated.
32 devices in a mesh: groups: 2 (over x), dp: 2 (over core), tensor: 8 (over z, y).
Axes of the slice: x: 2, y: 2, z: 4, core: 2. Of those that a mesh axis runs over, the one named last changes fastest.
Arguments:
- tokens: bfloat16 [512, 4608], P(('groups', 'dp', 'tensor')), parts along dimension 0, may hold values from -6 to 6
- gate_weight: bfloat16 [3584, 4608], P('tensor'), may hold values from -0.09375 to 0.09375
- up_weight: bfloat16 [3584, 4608], P('tensor'), may hold values from -0.09375 to 0.09375
- down_weight: bfloat16 [3584, 4608], P('tensor'), may hold values from -0.09375 to 0.09375
- format_codes: int32 [3, 3584], P(None, 'tensor'), may hold values from 0 to 1
- scale_exponents: int32 [3, 3584], P(None, 'tensor'), may hold values from 6 to 16, as said below
Outputs:
- mixed: bfloat16 [512, 4608], P(('groups', 'dp', 'tensor')), parts along dimension 0
There are 2 independent parts, one for each index of `groups`. A program takes and returns all parts, laid end to end along the dimension named above; an argument that names none is the same for every part. Nothing has to cross between parts.
Inputs may be any that keep to these rules, and one draw needn't show every extreme that they name: `scale_exponents`: each exponent minus (7 + 8 times its format code) is -1, 0 or 1.
All inputs are finite; a program needn't handle non-finite values.
Results may differ from a plain program's by a relative error of at most 0.0049.
Values may be sent and summed in bfloat16 or wider, within the bound.
A program may use at most 128 MiB of HBM per device.

v0:
```python
import jax
import jax.numpy as jnp
from jax import lax
from jax.sharding import PartitionSpec as P


def dequant_factors(format_codes, scale_exponents):
    offset = scale_exponents - (7 + 8 * format_codes)
    return jnp.exp2(offset.astype(jnp.float32))


def project_rows(rows, weight):
    return lax.dot_general(
        rows, weight, (((1,), (1,)), ((), ())), preferred_element_type=jnp.float32
    )


def on_device(tokens, gate_weight, up_weight, down_weight, format_codes, scale_exponents):
    factor = dequant_factors(format_codes, scale_exponents)
    scaled_down = (down_weight.astype(jnp.float32) * factor[2][:, None]).astype(jnp.bfloat16)
    gathered = lax.all_gather(tokens, "tensor", axis=0, tiled=True)
    gate = project_rows(gathered, gate_weight) * factor[0][None, :]
    up_part = project_rows(gathered, up_weight) * factor[1][None, :]
    hidden = (jax.nn.gelu(gate, approximate=True) * up_part).astype(jnp.bfloat16)
    return lax.psum_scatter(
        jnp.dot(hidden, scaled_down, preferred_element_type=jnp.float32),
        "tensor",
        scatter_dimension=0,
        tiled=True,
    ).astype(jnp.bfloat16)


def solution(mesh):
    return jax.shard_map(
        on_device,
        mesh=mesh,
        in_specs=(
            P(("groups", "dp", "tensor"), None),
            P("tensor", None),
            P("tensor", None),
            P("tensor", None),
            P(None, "tensor"),
            P(None, "tensor"),
        ),
        out_specs=P(("groups", "dp", "tensor"), None),
        check_vma=False,
    )
```

profile of v0, /device:TPU:0, one launch (start us, length us, event | category | flops | bytes accessed | tf_op | source)
XLA Modules:
  0.0 141.8 jit_solution(4148574959737134752)
XLA Ops:
  6.5 0.0 all-gather.2.cloned.1.call-start
  6.5 0.7 all-gather.2.cloned.1.call-update
  7.3 0.0 reduce-scatter.2.cloned.1.call-start
  7.3 0.7 multiply_exponential_fusion
  8.0 45.3 %all-gather.2.cloned.1.call-done = bf16[128,4608]{1,0:T(8,128)(2,1)} async-done(((bf16[16,4608]{1,0:T(8,128)(2,1)}), bf16[128,4608]{1,0:T(8,128)(2,1)}) %all-gather.2.cloned.1.call-update) | async-done | bytes 1179664 | tf_op jit(solution)/shard_map/all_gather | solution.py:21
  53.3 0.0 copy-start
  53.3 3.9 %fusion.10 = f32[128,448]{0,1:T(8,128)S(1)} fusion(bf16[128,4608]{1,0:T(8,128)(2,1)} %all-gather.2.cloned.1.call-done, bf16[448,4608]{1,0:T(8,128)(2,1)} %param.7, f32[448]{0:T(512)S(1)} %bitcast.7), kind=kOutput, calls=%fused_computation.14 | convolution fusion | flops 528998400 | bytes 5539584 | tf_op jit(solution)/shard_map/dot_general | solution.py:13
  57.2 0.0 copy-done
  57.2 8.1 %fusion = f32[128,4608]{1,0:T(8,128)} fusion(bf16[448,4608]{1,0:T(8,128)(2,1)} %param.9, f32[448]{0:T(512)S(1)} %bitcast.9, f32[128,448]{0,1:T(8,128)S(1)} %fusion.10, bf16[128,4608]{1,0:T(8,128)(2,1)S(1)} %copy-done, bf16[448,4608]{1,0:T(8,128)(2,1)} %param.8, f32[448]{0:T(512)S(1)} %bitcast.8), kind=kOutput, calls=%fused_computation.1 | convolution fusion | flops 1063329792 | bytes 12029440 | tf_op jit(solution)/shard_map/dot_general | solution.py:26
  65.3 0.0 reduce-scatter.2.cloned.1.call-update
  65.3 68.1 %reduce-scatter.2.cloned.1.call-done = f32[16,4608]{1,0:T(8,128)} async-done(((f32[128,4608]{1,0:T(8,128)}), f32[16,4608]{1,0:T(8,128)}) %reduce-scatter.2.cloned.1.call-update) | async-done | bytes 294928 | tf_op jit(solution)/shard_map/reduce_scatter | solution.py:25
  133.3 1.6 %convert_element_type.19 = bf16[16,4608]{1,0:T(8,128)(2,1)} convert(f32[16,4608]{1,0:T(8,128)} %reduce-scatter.2.cloned.1.call-done) | non-fusion elementwise | flops 73728 | bytes 442368 | tf_op jit(solution)/shard_map/convert_element_type | solution.py:30
  (1 shorter events, 0.0 us)
Async XLA Ops:
  6.5 46.8 %all-gather.2.cloned.1.call-start = ((), (), s32[]{:S(2)}) async-start(), calls=%async_computation.1 | async-start | bytes 1327104 | tf_op jit(solution)/shard_map/all_gather | solution.py:21
  7.3 126.1 %reduce-scatter.2.cloned.1.call-start = ((), (), s32[]{:S(2)}) async-start(), calls=%async_computation.2 | async-start | bytes 2654208 | tf_op jit(solution)/shard_map/reduce_scatter | solution.py:25
  53.3 3.9 %copy-start = (bf16[128,4608]{1,0:T(8,128)(2,1)S(1)}, bf16[128,4608]{1,0:T(8,128)(2,1)}, u32[]{:S(2)}) copy-start(bf16[128,4608]{1,0:T(8,128)(2,1)} %all-gather.2.cloned.1.call-done) | copy-start | bytes 3538948
Sparse Core Ops, SparseCore 0:
  9.5 43.7 all-gather.1
  65.4 67.8 reduce-scatter.1
where the time goes:
time: 142 us
  waiting for transfers between devices  114 us (80%)
  between operations  13.4 us (9%)
  matrix products  11.9 us (8%)
  other arithmetic  2.36 us (2%)
    reduce_scatter x1, waiting for transfers between devices, on_device(): lax.psum_scatter(jnp.dot(hidden, scaled_down, preferred_element_type=jnp....  68.1 us
    all_gather x1, waiting for transfers between devices, on_device(): gathered = lax.all_gather(tokens, 'tensor', axis=0, tiled=True)  45.3 us
    dot_general x1, matrix products, on_device(): jnp.dot(hidden, scaled_down, preferred_element_type=jnp.float32)  8.06 us
    dot_general x1, matrix products, project_rows(): lax.dot_general(rows, weight, (((1,), (1,)), ((), ())), preferred_element...  3.85 us
  transfers between devices with their start and end apart: 2, of which 2 were waited for; matrix products, arithmetic and copies ran while one was open for 1% of the time, Pallas kernels for 0%

commit v1 on v0

v1 whole, which is shorter than its diff:
```python
import functools
import math

import jax
import jax.numpy as jnp
from jax import lax
from jax.experimental import pallas as pl
from jax.experimental.pallas import tpu as pltpu
from jax.sharding import PartitionSpec as P

MESH = pl.DeviceIdType.MESH
F32 = jnp.float32
BF16 = jnp.bfloat16


def lines_of(n):
    inner = math.isqrt(n)
    while n % inner:
        inner -= 1
    return n // inner, inner


def kernel(
    A, B, tokens, gate_w, up_w, down_w, codes, exps, out,
    tok, wg, wu, wd, hid, part, own, sbuf, ybuf, rbuf, lbuf,
    w_sem, ag_recv, ag_r, ag_l, ag_y, y_send, y_recv, c_send, r_recv, l_recv,
):
    me = lax.axis_index("tensor")
    a, b = me // B, lax.rem(me, B)
    rows, D = tokens.shape
    has_left, has_right = a > 0, a < A - 1

    def dev(za, yb):
        return {"tensor": za * B + yb}

    def rcopy(src, dst, ssem, rsem, device):
        return pltpu.make_async_remote_copy(
            src_ref=src, dst_ref=dst, send_sem=ssem, recv_sem=rsem,
            device_id=device, device_id_type=MESH,
        )

    loads = [
        pltpu.make_async_copy(src, dst, w_sem.at[i])
        for i, (src, dst) in enumerate(((gate_w, wg), (up_w, wu), (down_w, wd)))
    ]
    for load in loads:
        load.start()

    barrier = pltpu.get_barrier_semaphore()
    partners = [lax.rem(b + o, B) for o in range(1, B)]
    for p in partners:
        pl.semaphore_signal(barrier, inc=1, device_id=dev(a, p), device_id_type=MESH)

    @pl.when(has_left)
    def _():
        pl.semaphore_signal(barrier, inc=1, device_id=dev(a - 1, b), device_id_type=MESH)

    @pl.when(has_right)
    def _():
        pl.semaphore_signal(barrier, inc=1, device_id=dev(a + 1, b), device_id_type=MESH)

    peers = B - 1 + jnp.minimum(a, 1) + jnp.minimum(A - 1 - a, 1)
    pl.semaphore_wait(barrier, peers)

    def ag_right(t, src):
        return rcopy(src, tok.at[b, t], ag_r.at[t], ag_recv.at[b, t], dev(a + 1, b))

    def ag_left(t, src):
        return rcopy(src, tok.at[b, t], ag_l.at[t], ag_recv.at[b, t], dev(a - 1, b))

    def ag_across(t, o, src):
        return rcopy(src, tok.at[b, t], ag_y.at[o - 1, t], ag_recv.at[b, t], dev(a, partners[o - 1]))

    def ag_wait(line, t):
        rcopy(tok.at[line, t], tok.at[line, t], ag_r.at[t], ag_recv.at[line, t], dev(a, partners[0])).wait_recv()

    @pl.when(has_right)
    def _():
        ag_right(a, tokens).start()

    @pl.when(has_left)
    def _():
        ag_left(a, tokens).start()

    for o in range(1, B):
        ag_across(a, o, tokens).start()
    tok[b, a] = tokens[...]

    for s in range(1, A):
        t_left, t_right = a - s, a + s

        @pl.when(t_left >= 0)
        def _():
            ag_wait(b, t_left)

            @pl.when(has_right)
            def _():
                ag_right(t_left, tok.at[b, t_left]).start()

            for o in range(1, B):
                ag_across(t_left, o, tok.at[b, t_left]).start()

        @pl.when(t_right < A)
        def _():
            ag_wait(b, t_right)

            @pl.when(has_left)
            def _():
                ag_left(t_right, tok.at[b, t_right]).start()

            for o in range(1, B):
                ag_across(t_right, o, tok.at[b, t_right]).start()

    offset = exps[...] - (7 + 8 * codes[...])
    factor = jnp.where(offset < 0, 0.5, jnp.where(offset > 0, 2.0, 1.0)).astype(F32)

    def project(line):
        x = tok[line].reshape(A * rows, D)
        dims = (((1,), (1,)), ((), ()))
        gate = lax.dot_general(x, wg[...], dims, preferred_element_type=F32) * factor[0:1, :]
        up = lax.dot_general(x, wu[...], dims, preferred_element_type=F32) * factor[1:2, :]
        h = (jax.nn.gelu(gate, approximate=True) * up).astype(BF16)
        hid[line] = (h.astype(F32) * factor[2:3, :]).astype(BF16)

    loads[0].wait()
    loads[1].wait()
    project(b)
    loads[2].wait()

    def y_copy(t, o):
        return rcopy(
            part.at[partners[o - 1], t], ybuf.at[o - 1, t],
            y_send.at[o - 1, t], y_recv.at[o - 1, t], dev(a, partners[o - 1]),
        )

    def by_distance(body):
        for d in range(A - 1, 0, -1):
            for t in (a + d, a - d):
                @pl.when((t >= 0) & (t < A))
                def _():
                    body(t)
        body(a)

    for o in range(1, B):
        line = partners[o - 1]
        for t in range(A):
            ag_wait(line, t)
        project(line)
        y = jnp.dot(hid[line], wd[...], preferred_element_type=F32)
        part[line] = y.astype(BF16).reshape(A, rows, D)
        by_distance(lambda t: y_copy(t, o).start())

    own[...] = jnp.dot(hid[b], wd[...], preferred_element_type=F32).reshape(A, rows, D)

    def right_copy(t):
        return rcopy(sbuf.at[t], rbuf.at[t], c_send.at[t], r_recv.at[t], dev(a + 1, b))

    def left_copy(t):
        return rcopy(sbuf.at[t], lbuf.at[t], c_send.at[t], l_recv.at[t], dev(a - 1, b))

    def gather_y(t):
        total = own[t]
        for o in range(1, B):
            y_copy(t, o).wait_recv()
            total += ybuf[o - 1, t].astype(F32)
        return total

    for d in range(A - 1, 0, -1):
        for right in (True, False):
            t = a + d if right else a - d

            @pl.when((t < A) if right else (t >= 0))
            def _():
                own[t] = gather_y(t)

                @pl.when(has_left if right else has_right)
                def _():
                    if right:
                        right_copy(t).wait_recv()
                        own[t] += rbuf[t].astype(F32)
                    else:
                        left_copy(t).wait_recv()
                        own[t] += lbuf[t].astype(F32)

                sbuf[t] = own[t].astype(BF16)
                (right_copy(t) if right else left_copy(t)).start()

    own[a] = gather_y(a)

    @pl.when(has_left)
    def _():
        right_copy(a).wait_recv()
        own[a] += rbuf[a].astype(F32)

    @pl.when(has_right)
    def _():
        left_copy(a).wait_recv()
        own[a] += lbuf[a].astype(F32)

    out[...] = own[a].astype(out.dtype)

    for t in range(A):
        @pl.when(has_right & (t <= a))
        def _():
            ag_right(t, tokens).wait_send()

        @pl.when(has_left & (t >= a))
        def _():
            ag_left(t, tokens).wait_send()

        for o in range(1, B):
            ag_across(t, o, tokens).wait_send()
            y_copy(t, o).wait_send()

        @pl.when(t != a)
        def _():
            right_copy(t).wait_send()


def on_device(n, tokens, gate_weight, up_weight, down_weight, format_codes, scale_exponents):
    A, B = lines_of(n)
    rows, D = tokens.shape
    hidden = gate_weight.shape[0]
    vmem = pl.BlockSpec(memory_space=pltpu.VMEM)
    hbm = pl.BlockSpec(memory_space=pl.ANY)
    dma = pltpu.SemaphoreType.DMA
    return pl.pallas_call(
        functools.partial(kernel, A, B),
        out_shape=jax.ShapeDtypeStruct((rows, D), BF16),
        in_specs=[vmem, hbm, hbm, hbm, vmem, vmem],
        out_specs=vmem,
        scratch_shapes=[
            pltpu.VMEM((B, A, rows, D), BF16),
            pltpu.VMEM((hidden, D), BF16),
            pltpu.VMEM((hidden, D), BF16),
            pltpu.VMEM((hidden, D), BF16),
            pltpu.VMEM((B, A * rows, hidden), BF16),
            pltpu.VMEM((B, A, rows, D), BF16),
            pltpu.VMEM((A, rows, D), F32),
            pltpu.VMEM((A, rows, D), BF16),
            pltpu.VMEM((B - 1, A, rows, D), BF16),
            pltpu.VMEM((A, rows, D), BF16),
            pltpu.VMEM((A, rows, D), BF16),
            dma((3,)),
            dma((B, A)),
            dma((A,)),
            dma((A,)),
            dma((B - 1, A)),
            dma((B - 1, A)),
            dma((B - 1, A)),
            dma((A,)),
            dma((A,)),
            dma((A,)),
        ],
        compiler_params=pltpu.CompilerParams(
            collective_id=0, has_side_effects=True, vmem_limit_bytes=60 * 2**20
        ),
    )(tokens, gate_weight, up_weight, down_weight, format_codes, scale_exponents)


def solution(mesh):
    return jax.shard_map(
        functools.partial(on_device, mesh.shape["tensor"]),
        mesh=mesh,
        in_specs=(
            P(("groups", "dp", "tensor"), None),
            P("tensor", None),
            P("tensor", None),
            P("tensor", None),
            P(None, "tensor"),
            P(None, "tensor"),
        ),
        out_specs=P(("groups", "dp", "tensor"), None),
        check_vma=False,
    )
```

time: 142 us -> 45.5 us (0.32)
  waiting for transfers between devices: 114 us -> 0 us
  Pallas kernels: 0 us -> 43.7 us
  between operations: 13.4 us -> 0.01 us
  matrix products: 11.9 us -> 0 us
  other arithmetic: 2.36 us -> 0 us
  local copies, waits for them, and re-layouts: 0.01 us -> 1.58 us
    reduce_scatter x1 -> x0, waiting for transfers between devices: 68.1 us -> none  [on_device(): lax.psum_scatter(jnp.dot(hidden, scaled_down, preferred_element_type=jnp....]
    all_gather x1 -> x0, waiting for transfers between devices: 45.3 us -> none  [on_device(): gathered = lax.all_gather(tokens, 'tensor', axis=0, tiled=True)]
    pallas_call x0 -> x1, Pallas kernels: none -> 43.7 us  [on_device(): pl.pallas_call(functools.partial(kernel, A, B), out_shape=jax.ShapeDtypeS...]
    dot_general x2 -> x0, matrix products: 11.9 us -> none  [the longest x1 8.06 us: on_device(): jnp.dot(hidden, scaled_down, preferred_element_type=jnp.float32)]
    convert_element_type x1 -> x0, other arithmetic: 1.64 us -> none  [on_device(): return lax.psum_scatter(jnp.dot(hidden, scaled_down, preferred_element_ty...]
    unnamed x2 -> x1, local copies, waits for them, and re-layouts: 0.01 us -> 1.58 us
  transfers between devices with their start and end apart: 2 -> 0, of which waited for: 2 -> 0; matrix products, arithmetic and copies ran while one was open for 1% -> 0% of each run, Pallas kernels for 0% -> 0%
where the time goes in v1:
time: 45.5 us; the launch traced here: 45.3 us
  Pallas kernels  43.7 us (96%)
  local copies, waits for them, and re-layouts  1.58 us (3%)
    pallas_call x1, Pallas kernels, on_device(): pl.pallas_call(functools.partial(kernel, A, B), out_shape=jax.ShapeDtypeS...  43.7 us
    unnamed x1, local copies, waits for them, and re-layouts  1.58 us

profile of v1, /device:TPU:0, one launch (start us, length us, event | category | flops | bytes accessed | tf_op | source)
XLA Modules:
  0.0 45.3 jit_solution(235747798934827657)
XLA Ops:
  0.0 43.7 %shard_map.64 = bf16[16,4608]{1,0:T(8,128)(2,1)} custom-call(bf16[16,4608]{1,0:T(8,128)(2,1)} %tokens.1, bf16[448,4608]{1,0:T(8,128)(2,1)} %gate_w.1, bf16[448,4608]{1,0:T(8,128)(2,1)} %up_w.1, bf16[448,4608]{1,0:T(8,128)(2,1)} %down_w.1, s32[3,448]{1,0:T(4,128)} %codes.1, s32[3,448]{1,0:T(4,128)} %exps.1), custom_call_target="tpu_custom_call" | custom-call | tf_op jit(solution)/shard_map/pallas_call | solution.py:227
  43.7 1.6 %copy.8 = bf16[16,4608]{1,0:T(8,128)(2,1)} copy(bf16[16,4608]{1,0:T(8,128)(2,1)} %shard_map.64) | data formatting | bytes 294912

commit v2 on v1

v2 whole, which is shorter than its diff:
```python
import functools
import math

import jax
import jax.numpy as jnp
from jax import lax
from jax.experimental import pallas as pl
from jax.experimental.pallas import tpu as pltpu
from jax.sharding import PartitionSpec as P

MESH = pl.DeviceIdType.MESH
F32 = jnp.float32
BF16 = jnp.bfloat16


def lines_of(n):
    inner = math.isqrt(n)
    while n % inner:
        inner -= 1
    return n // inner, inner


def kernel(
    A, B, C, tokens, gate_w, up_w, down_w, codes_in, exps_in, out,
    tok, wg, wu, wd, codes, exps, hid, part, own, sbuf, ybuf, rbuf, lbuf,
    w_sem, tok_sem, ag_recv, ag_r, ag_l, ag_y, y_send, y_recv, c_send, r_recv, l_recv,
):
    me = lax.axis_index("tensor")
    a, b = me // B, lax.rem(me, B)
    rows, D = tokens.shape
    width = D // C
    has_left, has_right = a > 0, a < A - 1

    def cols(c):
        return pl.ds(c * width, width)

    def dev(za, yb):
        return {"tensor": za * B + yb}

    def rcopy(src, dst, ssem, rsem, device):
        return pltpu.make_async_remote_copy(
            src_ref=src, dst_ref=dst, send_sem=ssem, recv_sem=rsem,
            device_id=device, device_id_type=MESH,
        )

    barrier = pltpu.get_barrier_semaphore()
    partners = [lax.rem(b + o, B) for o in range(1, B)]
    for p in partners:
        pl.semaphore_signal(barrier, inc=1, device_id=dev(a, p), device_id_type=MESH)

    @pl.when(has_left)
    def _():
        pl.semaphore_signal(barrier, inc=1, device_id=dev(a - 1, b), device_id_type=MESH)

    @pl.when(has_right)
    def _():
        pl.semaphore_signal(barrier, inc=1, device_id=dev(a + 1, b), device_id_type=MESH)

    own_tokens = pltpu.make_async_copy(tokens, tok.at[b, a], tok_sem)
    own_tokens.start()
    loads = [
        pltpu.make_async_copy(src, dst, w_sem.at[i])
        for i, (src, dst) in enumerate(
            ((codes_in, codes), (exps_in, exps), (gate_w, wg), (up_w, wu), (down_w, wd))
        )
    ]
    for load in loads:
        load.start()

    peers = B - 1 + jnp.minimum(a, 1) + jnp.minimum(A - 1 - a, 1)
    pl.semaphore_wait(barrier, peers)

    def ag_copy(t, c, src, ssem, device):
        return rcopy(
            src.at[:, cols(c)], tok.at[b, t, :, cols(c)], ssem, ag_recv.at[b, t, c], device
        )

    def ag_right(t, c, src):
        return ag_copy(t, c, src, ag_r.at[t, c], dev(a + 1, b))

    def ag_left(t, c, src):
        return ag_copy(t, c, src, ag_l.at[t, c], dev(a - 1, b))

    def ag_across(t, c, o, src):
        return ag_copy(t, c, src, ag_y.at[o - 1, t, c], dev(a, partners[o - 1]))

    def ag_wait(line, t, c):
        block = tok.at[line, t, :, cols(c)]
        rcopy(block, block, ag_r.at[t, c], ag_recv.at[line, t, c], dev(a, partners[0])).wait_recv()

    for c in range(C):
        @pl.when(has_right)
        def _():
            ag_right(a, c, tokens).start()

        @pl.when(has_left)
        def _():
            ag_left(a, c, tokens).start()

        for o in range(1, B):
            ag_across(a, c, o, tokens).start()

    for s in range(1, A):
        t_left, t_right = a - s, a + s
        for c in range(C):
            @pl.when(t_left >= 0)
            def _():
                ag_wait(b, t_left, c)

                @pl.when(has_right)
                def _():
                    ag_right(t_left, c, tok.at[b, t_left]).start()

                for o in range(1, B):
                    ag_across(t_left, c, o, tok.at[b, t_left]).start()

            @pl.when(t_right < A)
            def _():
                ag_wait(b, t_right, c)

                @pl.when(has_left)
                def _():
                    ag_left(t_right, c, tok.at[b, t_right]).start()

                for o in range(1, B):
                    ag_across(t_right, c, o, tok.at[b, t_right]).start()

    loads[0].wait()
    loads[1].wait()
    offset = exps[...] - (7 + 8 * codes[...])
    factor = jnp.where(offset < 0, 0.5, jnp.where(offset > 0, 2.0, 1.0)).astype(F32)

    def project(line):
        x = tok[line].reshape(A * rows, D)
        dims = (((1,), (1,)), ((), ()))
        gate = lax.dot_general(x, wg[...], dims, preferred_element_type=F32) * factor[0:1, :]
        up = lax.dot_general(x, wu[...], dims, preferred_element_type=F32) * factor[1:2, :]
        h = (jax.nn.gelu(gate, approximate=True) * up).astype(BF16)
        hid[line] = (h.astype(F32) * factor[2:3, :]).astype(BF16)

    own_tokens.wait()
    loads[2].wait()
    loads[3].wait()
    project(b)
    loads[4].wait()

    def y_copy(t, c, o):
        return rcopy(
            part.at[partners[o - 1], t, :, cols(c)], ybuf.at[o - 1, t, :, cols(c)],
            y_send.at[o - 1, t, c], y_recv.at[o - 1, t, c], dev(a, partners[o - 1]),
        )

    def by_distance(body):
        for d in range(A - 1, 0, -1):
            for t in (a + d, a - d):
                @pl.when((t >= 0) & (t < A))
                def _():
                    body(t)
        body(a)

    for o in range(1, B):
        line = partners[o - 1]
        for t in range(A):
            for c in range(C):
                ag_wait(line, t, c)
        project(line)
        y = jnp.dot(hid[line], wd[...], preferred_element_type=F32)
        part[line] = y.astype(BF16).reshape(A, rows, D)

        def send(t):
            for c in range(C):
                y_copy(t, c, o).start()

        by_distance(send)

    own[...] = jnp.dot(hid[b], wd[...], preferred_element_type=F32).reshape(A, rows, D)

    def right_copy(t, c):
        return rcopy(
            sbuf.at[t, :, cols(c)], rbuf.at[t, :, cols(c)],
            c_send.at[t, c], r_recv.at[t, c], dev(a + 1, b),
        )

    def left_copy(t, c):
        return rcopy(
            sbuf.at[t, :, cols(c)], lbuf.at[t, :, cols(c)],
            c_send.at[t, c], l_recv.at[t, c], dev(a - 1, b),
        )

    def add_y(t, c):
        total = own[t, :, cols(c)]
        for o in range(1, B):
            y_copy(t, c, o).wait_recv()
            total += ybuf[o - 1, t, :, cols(c)].astype(F32)
        own[t, :, cols(c)] = total

    def add_left(t, c):
        @pl.when(has_left)
        def _():
            right_copy(t, c).wait_recv()
            own[t, :, cols(c)] += rbuf[t, :, cols(c)].astype(F32)

    def add_right(t, c):
        @pl.when(has_right)
        def _():
            left_copy(t, c).wait_recv()
            own[t, :, cols(c)] += lbuf[t, :, cols(c)].astype(F32)

    for d in range(A - 1, 0, -1):
        for c in range(C):
            @pl.when(a + d < A)
            def _():
                t = a + d
                add_y(t, c)
                add_left(t, c)
                sbuf[t, :, cols(c)] = own[t, :, cols(c)].astype(BF16)
                right_copy(t, c).start()

            @pl.when(a - d >= 0)
            def _():
                t = a - d
                add_y(t, c)
                add_right(t, c)
                sbuf[t, :, cols(c)] = own[t, :, cols(c)].astype(BF16)
                left_copy(t, c).start()

    for c in range(C):
        add_y(a, c)
        add_left(a, c)
        add_right(a, c)
        out[:, cols(c)] = own[a, :, cols(c)].astype(out.dtype)

    for t in range(A):
        for c in range(C):
            @pl.when(has_right & (t <= a))
            def _():
                ag_right(t, c, tokens).wait_send()

            @pl.when(has_left & (t >= a))
            def _():
                ag_left(t, c, tokens).wait_send()

            for o in range(1, B):
                ag_across(t, c, o, tokens).wait_send()
                y_copy(t, c, o).wait_send()

            @pl.when(t != a)
            def _():
                right_copy(t, c).wait_send()


def on_device(n, tokens, gate_weight, up_weight, down_weight, format_codes, scale_exponents):
    A, B = lines_of(n)
    C = 4
    rows, D = tokens.shape
    hidden = gate_weight.shape[0]
    vmem = pl.BlockSpec(memory_space=pltpu.VMEM)
    hbm = pl.BlockSpec(memory_space=pl.ANY)
    dma = pltpu.SemaphoreType.DMA
    return pl.pallas_call(
        functools.partial(kernel, A, B, C),
        out_shape=jax.ShapeDtypeStruct((rows, D), BF16),
        in_specs=[hbm] * 6,
        out_specs=vmem,
        scratch_shapes=[
            pltpu.VMEM((B, A, rows, D), BF16),
            pltpu.VMEM((hidden, D), BF16),
            pltpu.VMEM((hidden, D), BF16),
            pltpu.VMEM((hidden, D), BF16),
            pltpu.VMEM(format_codes.shape, jnp.int32),
            pltpu.VMEM(scale_exponents.shape, jnp.int32),
            pltpu.VMEM((B, A * rows, hidden), BF16),
            pltpu.VMEM((B, A, rows, D), BF16),
            pltpu.VMEM((A, rows, D), F32),
            pltpu.VMEM((A, rows, D), BF16),
            pltpu.VMEM((B - 1, A, rows, D), BF16),
            pltpu.VMEM((A, rows, D), BF16),
            pltpu.VMEM((A, rows, D), BF16),
            dma((5,)),
            dma(()),
            dma((B, A, C)),
            dma((A, C)),
            dma((A, C)),
            dma((B - 1, A, C)),
            dma((B - 1, A, C)),
            dma((B - 1, A, C)),
            dma((A, C)),
            dma((A, C)),
            dma((A, C)),
        ],
        compiler_params=pltpu.CompilerParams(
            collective_id=0, has_side_effects=True, vmem_limit_bytes=60 * 2**20
        ),
    )(tokens, gate_weight, up_weight, down_weight, format_codes, scale_exponents)


def solution(mesh):
    return jax.shard_map(
        functools.partial(on_device, mesh.shape["tensor"]),
        mesh=mesh,
        in_specs=(
            P(("groups", "dp", "tensor"), None),
            P("tensor", None),
            P("tensor", None),
            P("tensor", None),
            P(None, "tensor"),
            P(None, "tensor"),
        ),
        out_specs=P(("groups", "dp", "tensor"), None),
        check_vma=False,
    )
```

time: 45.5 us -> 41 us (0.901)
  Pallas kernels: 43.7 us -> 39.3 us
    pallas_call x1, Pallas kernels: 43.7 us -> 39.3 us  [on_device(): pl.pallas_call(functools.partial(kernel, A, B, C), out_shape=jax.ShapeDty...]
where the time goes in v2:
time: 41 us; the launch traced here: 40.9 us
  Pallas kernels  39.3 us (96%)
  local copies, waits for them, and re-layouts  1.58 us (4%)
    pallas_call x1, Pallas kernels, on_device(): pl.pallas_call(functools.partial(kernel, A, B, C), out_shape=jax.ShapeDty...  39.3 us
    unnamed x1, local copies, waits for them, and re-layouts  1.58 us

profile of v2, /device:TPU:0, one launch (start us, length us, event | category | flops | bytes accessed | tf_op | source)
XLA Modules:
  0.0 40.9 jit_solution(9552772542762276888)
XLA Ops:
  0.0 39.3 %shard_map.64 = bf16[16,4608]{1,0:T(8,128)(2,1)} custom-call(bf16[16,4608]{1,0:T(8,128)(2,1)} %tokens.1, bf16[448,4608]{1,0:T(8,128)(2,1)} %gate_w.1, bf16[448,4608]{1,0:T(8,128)(2,1)} %up_w.1, bf16[448,4608]{1,0:T(8,128)(2,1)} %down_w.1, s32[3,448]{1,0:T(4,128)} %codes_in.1, s32[3,448]{1,0:T(4,128)} %exps_in.1), custom_call_target="tpu_custom_call" | custom-call | tf_op jit(solution)/shard_map/pallas_call | solution.py:260
  39.3 1.6 %copy.8 = bf16[16,4608]{1,0:T(8,128)(2,1)} copy(bf16[16,4608]{1,0:T(8,128)(2,1)} %shard_map.64) | data formatting | bytes 294912

commit v3 on v2

--- a/solution.py
+++ b/solution.py
@@ -100,8 +100,29 @@
         for o in range(1, B):
             ag_across(a, c, o, tokens).start()
 
+    dims = (((1,), (1,)), ((), ()))
+
+    def project(line, c):
+        x = tok[line, :, :, cols(c)].reshape(A * rows, width)
+        return (
+            lax.dot_general(x, wg[:, cols(c)], dims, preferred_element_type=F32),
+            lax.dot_general(x, wu[:, cols(c)], dims, preferred_element_type=F32),
+        )
+
+    def finish(line, gate, up):
+        offset = exps[...] - (7 + 8 * codes[...])
+        factor = jnp.where(offset < 0, 0.5, jnp.where(offset > 0, 2.0, 1.0)).astype(F32)
+        gate, up = gate * factor[0:1, :], up * factor[1:2, :]
+        h = (jax.nn.gelu(gate, approximate=True) * up).astype(BF16)
+        hid[line] = (h.astype(F32) * factor[2:3, :]).astype(BF16)
+
+    gate = up = 0.0
     for s in range(1, A):
         t_left, t_right = a - s, a + s
+        if s == A - 1:
+            own_tokens.wait()
+            for load in loads[:4]:
+                load.wait()
         for c in range(C):
             @pl.when(t_left >= 0)
             def _():
@@ -125,24 +146,12 @@
                 for o in range(1, B):
                     ag_across(t_right, c, o, tok.at[b, t_right]).start()
 
-    loads[0].wait()
-    loads[1].wait()
-    offset = exps[...] - (7 + 8 * codes[...])
-    factor = jnp.where(offset < 0, 0.5, jnp.where(offset > 0, 2.0, 1.0)).astype(F32)
-
-    def project(line):
-        x = tok[line].reshape(A * rows, D)
-        dims = (((1,), (1,)), ((), ()))
-        gate = lax.dot_general(x, wg[...], dims, preferred_element_type=F32) * factor[0:1, :]
-        up = lax.dot_general(x, wu[...], dims, preferred_element_type=F32) * factor[1:2, :]
-        h = (jax.nn.gelu(gate, approximate=True) * up).astype(BF16)
-        hid[line] = (h.astype(F32) * factor[2:3, :]).astype(BF16)
-
-    own_tokens.wait()
-    loads[2].wait()
-    loads[3].wait()
-    project(b)
-    loads[4].wait()
+            if s == A - 1:
+                gate_c, up_c = project(b, c)
+                gate += gate_c
+                up += up_c
+
+    finish(b, gate, up)
 
     def y_copy(t, c, o):
         return rcopy(
@@ -153,19 +162,29 @@
     def by_distance(body):
         for d in range(A - 1, 0, -1):
             for t in (a + d, a - d):
-                @pl.when((t >= 0) & (t < A))
+                @pl.when((t >= 0) & (t < A) & (t != far))
                 def _():
                     body(t)
-        body(a)
+        pl.when(a != far)(lambda: body(a))
+
+    far = jnp.where(2 * a < A, A - 1, 0)
 
     for o in range(1, B):
         line = partners[o - 1]
-        for t in range(A):
-            for c in range(C):
+        gate = up = 0.0
+        for c in range(C):
+            for t in range(A):
                 ag_wait(line, t, c)
-        project(line)
-        y = jnp.dot(hid[line], wd[...], preferred_element_type=F32)
-        part[line] = y.astype(BF16).reshape(A, rows, D)
+            gate_c, up_c = project(line, c)
+            gate += gate_c
+            up += up_c
+        finish(line, gate, up)
+        if o == 1:
+            loads[4].wait()
+        for c in range(C):
+            y = jnp.dot(hid[line], wd[:, cols(c)], preferred_element_type=F32)
+            part[line, :, :, cols(c)] = y.astype(BF16).reshape(A, rows, width)
+            y_copy(far, c, o).start()
 
         def send(t):
             for c in range(C):
@@ -251,7 +270,7 @@
 
 def on_device(n, tokens, gate_weight, up_weight, down_weight, format_codes, scale_exponents):
     A, B = lines_of(n)
-    C = 4
+    C = 4 if n <= 8 else 2
     rows, D = tokens.shape
     hidden = gate_weight.shape[0]
     vmem = pl.BlockSpec(memory_space=pltpu.VMEM)
@@ -259,7 +278,7 @@
     dma = pltpu.SemaphoreType.DMA
     return pl.pallas_call(
         functools.partial(kernel, A, B, C),
-        out_shape=jax.ShapeDtypeStruct((rows, D), BF16),
+        out_shape=pltpu.VMEM((rows, D), BF16),
         in_specs=[hbm] * 6,
         out_specs=vmem,
         scratch_shapes=[

time: 41 us -> 38.3 us (0.934)
  Pallas kernels: 39.3 us -> 37.5 us
  local copies, waits for them, and re-layouts: 1.58 us -> 0.66 us
    pallas_call x1, Pallas kernels: 39.3 us -> 37.5 us  [on_device(): pl.pallas_call(functools.partial(kernel, A, B, C), out_shape=pltpu.VMEM((...]
    unnamed x1, local copies, waits for them, and re-layouts: 1.58 us -> 0.66 us
where the time goes in v3:
time: 38.3 us; the launch traced here: 38.2 us
  Pallas kernels  37.5 us (98%)
  local copies, waits for them, and re-layouts  0.66 us (2%)
    pallas_call x1, Pallas kernels, on_device(): pl.pallas_call(functools.partial(kernel, A, B, C), out_shape=pltpu.VMEM((...  37.5 us

profile of v3, /device:TPU:0, one launch (start us, length us, event | category | flops | bytes accessed | tf_op | source)
XLA Modules:
  0.0 38.2 jit_solution(11706966211614069046)
XLA Ops:
  0.0 37.5 %shard_map.64 = bf16[16,4608]{1,0:T(8,128)(2,1)S(1)} custom-call(bf16[16,4608]{1,0:T(8,128)(2,1)} %tokens.1, bf16[448,4608]{1,0:T(8,128)(2,1)} %gate_w.1, bf16[448,4608]{1,0:T(8,128)(2,1)} %up_w.1, bf16[448,4608]{1,0:T(8,128)(2,1)} %down_w.1, s32[3,448]{1,0:T(4,128)} %codes_in.1, s32[3,448]{1,0:T(4,128)} %exps_in.1), custom_call_target="tpu_custom_call" | custom-call | tf_op jit(solution)/shard_map/pallas_call | solution.py:279
  37.5 0.7 %copy.8 = bf16[16,4608]{1,0:T(8,128)(2,1)} copy(bf16[16,4608]{1,0:T(8,128)(2,1)S(1)} %shard_map.64) | data formatting | bytes 294912

commit v4 on v3

--- a/solution.py
+++ b/solution.py
@@ -64,9 +64,6 @@
             ((codes_in, codes), (exps_in, exps), (gate_w, wg), (up_w, wu), (down_w, wd))
         )
     ]
-    for load in loads:
-        load.start()
-
     peers = B - 1 + jnp.minimum(a, 1) + jnp.minimum(A - 1 - a, 1)
     pl.semaphore_wait(barrier, peers)
 
@@ -99,6 +96,9 @@
 
         for o in range(1, B):
             ag_across(a, c, o, tokens).start()
+
+    for load in loads:
+        load.start()
 
     dims = (((1,), (1,)), ((), ()))
 

time: 38.3 us -> 38.3 us (level)
  no operation moved by 1% of the time
where the time goes in v4:
time: 38.3 us; the launch traced here: 38.2 us
  Pallas kernels  37.5 us (98%)
  local copies, waits for them, and re-layouts  0.66 us (2%)
    pallas_call x1, Pallas kernels, on_device(): pl.pallas_call(functools.partial(kernel, A, B, C), out_shape=pltpu.VMEM((...  37.5 us

profile of v4, /device:TPU:0, one launch (start us, length us, event | category | flops | bytes accessed | tf_op | source)
XLA Modules:
  0.0 38.2 jit_solution(9334304447590574865)
XLA Ops:
  0.0 37.5 %shard_map.64 = bf16[16,4608]{1,0:T(8,128)(2,1)S(1)} custom-call(bf16[16,4608]{1,0:T(8,128)(2,1)} %tokens.1, bf16[448,4608]{1,0:T(8,128)(2,1)} %gate_w.1, bf16[448,4608]{1,0:T(8,128)(2,1)} %up_w.1, bf16[448,4608]{1,0:T(8,128)(2,1)} %down_w.1, s32[3,448]{1,0:T(4,128)} %codes_in.1, s32[3,448]{1,0:T(4,128)} %exps_in.1), custom_call_target="tpu_custom_call" | custom-call | tf_op jit(solution)/shard_map/pallas_call | solution.py:279
  37.5 0.7 %copy.8 = bf16[16,4608]{1,0:T(8,128)(2,1)} copy(bf16[16,4608]{1,0:T(8,128)(2,1)S(1)} %shard_map.64) | data formatting | bytes 294912
